TPU v7x, 32 devices: a whole 2x2x4 slice. The times are simulated.
32 devices in a mesh: row: 4 (over x, core), col: 8 (over z, y).
Axes of the slice: x: 2, y: 2, z: 4, core: 2. Of those that a mesh axis runs over, the one named last changes fastest.
Arguments:
- panel_inverse: bfloat16 [2, 2, 2, 1024, 1024], P(None, None, None, ('row', 'col')), may hold values from -0.125 to 0.125
- panel_below: bfloat16 [2, 2, 1024, 1024], P(None, None, ('row', 'col')), may hold values from -0.25 to 0.25
- trail_factor: bfloat16 [2, 2, 2, 32768, 1024], P(None, None, None, ('row', 'col')), may hold values from -0.125 to 0.125
- first_rhs: bfloat16 [2, 2, 1024, 256], replicated, may hold values from -6 to 6
- second_rhs: bfloat16 [2, 2, 1024, 256], P(None, None, ('row', 'col')), may hold values from -6 to 6
- trail_rhs: bfloat16 [2, 2, 32768, 256], P(None, None, ('row', 'col')), may hold values from -6 to 6
- shape_tiles: float32 [2, 9, 2, 1024], P(None, None, None, ('row', 'col')), may hold values from -0.25 to 0.25
- element_vertices: int32 [2, 1024, 3], P(None, ('row', 'col')), may hold values from 0 to 255, all different within a row
- vertex_slot: int32 [256], replicated, may hold values from 0 to 255, each once
Outputs:
- panel_solution: bfloat16 [2, 2, 2, 1024, 256], P(None, None, None, ('row', 'col'))
- trail_update: bfloat16 [2, 2, 32768, 256], P(None, None, ('row', 'col'))
- vertex_gradient: float32 [3, 256], P(None, ('row', 'col'))
Inputs may be any that keep to these rules, and one draw needn't show every extreme that they name: `element_vertices`: each element names three different vertices, and every vertex is named by some element. `vertex_slot`: each slot is given to exactly one vertex.
All inputs are finite; a program needn't handle non-finite values.
Results may differ from a plain program's by a relative error of at most 0.0067.
Values may be sent and summed in bfloat16 or wider, within the bound.
A program may use at most 128 MiB of HBM per device.

v0:
```python
import jax
import jax.numpy as jnp
from jax import lax
from jax.sharding import PartitionSpec as P


def complex_rows(left_pair, right_pair, form):
    real_part = jnp.einsum(
        form, left_pair[0], right_pair[0], preferred_element_type=jnp.float32
    ) - jnp.einsum(form, left_pair[1], right_pair[1], preferred_element_type=jnp.float32)
    imag_part = jnp.einsum(
        form, left_pair[0], right_pair[1], preferred_element_type=jnp.float32
    ) + jnp.einsum(form, left_pair[1], right_pair[0], preferred_element_type=jnp.float32)
    return (real_part, imag_part)


def trail_terms(totals, factor_section, solution_parts):
    term_real, term_imag = complex_rows(
        (factor_section[:, 0], factor_section[:, 1]), solution_parts, "srn,sna->sra"
    )
    return (totals[0] - term_real, totals[1] - term_imag)


def couple_partials(panel_solution, shape_tiles):
    forward = panel_solution[0].astype(jnp.float32)
    adjoint = panel_solution[1].astype(jnp.float32)
    coupling_real = jnp.sum(forward[:, 0] * adjoint[:, 0] - forward[:, 1] * adjoint[:, 1], axis=-1)
    coupling_imag = jnp.sum(forward[:, 0] * adjoint[:, 1] + forward[:, 1] * adjoint[:, 0], axis=-1)
    return -(shape_tiles[0] * coupling_real - shape_tiles[1] * coupling_imag)


def spread_vertices(partials, element_vertices, vertex_slot, vertex_count):
    values = jnp.transpose(
        partials.reshape(3, 3, partials.shape[1], partials.shape[2]), (1, 2, 3, 0)
    )
    slots = vertex_slot[element_vertices]
    empty = jnp.zeros((3, vertex_count), jnp.float32)
    return empty.at[:, slots.reshape(-1)].add(values.reshape(3, -1))


def body(
    panel_inverse,
    panel_below,
    trail_factor,
    first_rhs,
    second_rhs,
    trail_rhs,
    shape_tiles,
    element_vertices,
    vertex_slot,
):
    form = "srn,sna->sra"
    first_parts = complex_rows(
        (panel_inverse[:, 0, 0], panel_inverse[:, 0, 1]), (first_rhs[:, 0], first_rhs[:, 1]), form
    )
    first_real = first_parts[0].astype(jnp.bfloat16)
    first_imag = first_parts[1].astype(jnp.bfloat16)
    own_rows = first_real.shape[1]
    own_right = second_rhs.astype(jnp.float32)
    below_real, below_imag = complex_rows(
        (panel_below[:, 0], panel_below[:, 1]), (first_real, first_imag), "sji,sja->sia"
    )
    offset = lax.axis_index(("row", "col")) * own_rows

    def embed_rows(negated, own_part):
        window = lax.dynamic_slice_in_dim(negated, offset, own_rows, 1) + own_part
        return lax.dynamic_update_slice_in_dim(negated, window, offset, 1)

    summed = lax.psum(
        (embed_rows(-below_real, own_right[:, 0]), embed_rows(-below_imag, own_right[:, 1])),
        ("row", "col"),
    )
    right_real = summed[0].astype(jnp.bfloat16)
    right_imag = summed[1].astype(jnp.bfloat16)
    second_parts = complex_rows(
        (panel_inverse[:, 1, 0], panel_inverse[:, 1, 1]), (right_real, right_imag), form
    )
    second_real = second_parts[0].astype(jnp.bfloat16)
    second_imag = second_parts[1].astype(jnp.bfloat16)
    initial = (trail_rhs[:, 0].astype(jnp.float32), trail_rhs[:, 1].astype(jnp.float32))
    first_factor = trail_factor[:, 0]
    second_factor = trail_factor[:, 1]
    totals = trail_terms(
        initial,
        first_factor,
        (
            lax.all_gather(first_real, ("row", "col"), axis=1, tiled=True),
            lax.all_gather(first_imag, ("row", "col"), axis=1, tiled=True),
        ),
    )
    totals = trail_terms(
        totals,
        second_factor,
        (
            lax.all_gather(second_real, ("row", "col"), axis=1, tiled=True),
            lax.all_gather(second_imag, ("row", "col"), axis=1, tiled=True),
        ),
    )
    trail_update = jnp.stack(totals, axis=1).astype(jnp.bfloat16)
    panel_solution = jnp.stack(
        [
            jnp.stack([first_real, first_imag], axis=1),
            jnp.stack([second_real, second_imag], axis=1),
        ],
        axis=1,
    )
    partials = couple_partials(panel_solution, shape_tiles)
    dense_local = spread_vertices(partials, element_vertices, vertex_slot, vertex_slot.shape[0])
    vertex_gradient = lax.psum_scatter(dense_local, ("row", "col"), scatter_dimension=1, tiled=True)
    return (panel_solution, trail_update, vertex_gradient)


def solution(mesh):
    return jax.shard_map(
        body,
        mesh=mesh,
        in_specs=(
            P(None, None, None, ("row", "col"), None),
            P(None, None, ("row", "col"), None),
            P(None, None, None, ("row", "col"), None),
            P(),
            P(None, None, ("row", "col"), None),
            P(None, None, ("row", "col"), None),
            P(None, None, None, ("row", "col")),
            P(None, ("row", "col"), None),
            P(),
        ),
        out_specs=(
            P(None, None, None, ("row", "col"), None),
            P(None, None, ("row", "col"), None),
            P(None, ("row", "col")),
        ),
        check_vma=False,
    )
```

profile of v0, /device:TPU:0, one launch (start us, length us, event | category | flops | bytes accessed | tf_op | source)
XLA Modules:
  0.0 260.8 jit_solution(4882548514613291878)
XLA Ops:
  7.3 1.7 fusion.18
  9.0 2.3 fusion.15
  11.6 0.9 fusion.14
  13.3 0.5 add_negate_fusion
  14.8 0.5 subtract_negate_fusion
  15.3 1.3 copy-done.2
  16.8 1.8 dynamic_update_slice.6
  18.6 1.1 dynamic_update_slice.7
  19.7 100.8 %all-reduce.3 = (bf16[2,1024,256]{1,2,0:T(8,128)(2,1)}, bf16[2,1024,256]{1,2,0:T(8,128)(2,1)S(1)}) all-reduce(f32[2,1024,256]{1,2,0:T(8,128)S(1)} %dynamic_update_slice.7, f32[2,1024,256]{1,2,0:T(8,128)} %dynamic_update_slice.6), channel_id=1, replica_groups=mesh['row'=4,'col'=8] {'row','col'}, use_global_device_ids=true, to_apply=%region_1.0 | all-reduce | flops 1048576 | bytes 6291456 | tf_op jit(solution)/shard_map/psum | solution.py:69
  120.5 1.4 fusion.32
  121.9 2.3 fusion.16
  124.7 1.1 fusion.17
  125.8 0.8 maximum_bitcast_fusion.1
  127.5 1.6 gather_fusion
  129.1 1.3 scatter_custom_fusion
  130.4 39.2 %all-reduce = f32[3,256]{0,1:T(8,128)S(1)} all-reduce(f32[3,256]{0,1:T(8,128)S(1)} %scatter_custom_fusion), channel_id=2, replica_groups=mesh['row'=4,'col'=8] {'row','col'}, use_global_device_ids=true, to_apply=%region_5.0.clone | all-reduce | flops 768 | bytes 6144
  169.6 0.7 copy.107
  170.2 11.8 %fusion.68 = (bf16[2,1,2,1024,1024]{4,3,2,1,0:T(8,128)(2,1)}, bf16[2,1,2,1024,1024]{4,3,2,1,0:T(8,128)(2,1)}) fusion(bf16[2,2,2,1024,1024]{4,3,2,1,0:T(8,128)(2,1)} %param.11), kind=kLoop, calls=%fused_computation.100 | loop fusion | bytes 33554432 | tf_op jit(solution)/shard_map/slice | solution.py:81
  182.2 0.5 copy.120
  182.7 0.5 copy.123
  183.3 0.7 copy.105
  183.9 11.7 %copy_bitcast_fusion = (bf16[2,2,1024,1024]{3,2,0,1:T(8,128)(2,1)}, bf16[2,2,1024,1024]{3,2,0,1:T(8,128)(2,1)}) fusion(bf16[2,1,2,1024,1024]{4,3,2,1,0:T(8,128)(2,1)} %get-tuple-element.20, bf16[2,1,2,1024,1024]{4,3,2,1,0:T(8,128)(2,1)} %get-tuple-element.19), kind=kLoop, calls=%fused_computation.2 | loop fusion | bytes 33554432 | tf_op jit(solution)/shard_map/squeeze | solution.py:82
  195.6 5.3 %fusion.3 = f32[2,256,1024]{2,1,0:T(8,128)} fusion(bf16[2,1024,256]{2,1,0:T(8,128)(2,1)} %all-gather.7.cloned.1.call-done, bf16[2,2,1024,1024]{3,2,0,1:T(8,128)(2,1)} %get-tuple-element.28), kind=kOutput, calls=%fused_computation.11 | convolution fusion | flops 1073741824 | bytes 7340032 | tf_op jit(solution)/shard_map/srn,sna->sra/dot_general | solution.py:10
  200.9 4.9 %fusion = f32[2,256,1024]{2,1,0:T(8,128)} fusion(bf16[2,1024,256]{2,1,0:T(8,128)(2,1)S(1)} %copy-done.20, bf16[2,2,1024,1024]{3,2,0,1:T(8,128)(2,1)} %get-tuple-element.28), kind=kOutput, calls=%fused_computation.8 | convolution fusion | flops 1073741824 | bytes 7340032 | tf_op jit(solution)/shard_map/srn,sna->sra/dot_general | solution.py:11
  205.9 5.4 %fusion.1 = f32[2,256,1024]{2,1,0:T(8,128)} fusion(bf16[2,1024,256]{2,1,0:T(8,128)(2,1)} %all-gather.5.cloned.1.call-done, bf16[2,2,1024,1024]{3,2,0,1:T(8,128)(2,1)} %get-tuple-element.28), kind=kOutput, calls=%fused_computation.9 | convolution fusion | flops 1073741824 | bytes 7340032 | tf_op jit(solution)/shard_map/srn,sna->sra/dot_general | solution.py:8
  211.2 5.0 %fusion.2 = f32[2,256,1024]{2,1,0:T(8,128)} fusion(bf16[2,1024,256]{2,1,0:T(8,128)(2,1)S(1)} %copy-done.21, bf16[2,2,1024,1024]{3,2,0,1:T(8,128)(2,1)} %get-tuple-element.28), kind=kOutput, calls=%fused_computation.10 | convolution fusion | flops 1073741824 | bytes 7340032 | tf_op jit(solution)/shard_map/srn,sna->sra/dot_general | solution.py:13
  216.2 5.3 %fusion.5 = f32[2,256,1024]{2,1,0:T(8,128)} fusion(bf16[2,1024,256]{2,1,0:T(8,128)(2,1)} %all-gather.9.cloned.1.call-done, bf16[2,2,1024,1024]{3,2,0,1:T(8,128)(2,1)} %get-tuple-element.27), kind=kOutput, calls=%fused_computation.13 | convolution fusion | flops 1073741824 | bytes 7340032 | tf_op jit(solution)/shard_map/srn,sna->sra/dot_general | solution.py:8
  221.5 17.5 %all-gather.11.cloned.1.call-done = bf16[2,1024,256]{2,1,0:T(8,128)(2,1)} async-done(((bf16[2,32,256]{2,1,0:T(8,128)(2,1)}), bf16[2,1024,256]{2,1,0:T(8,128)(2,1)}) %all-gather.11.cloned.1.call-update) | async-done | bytes 1048592 | tf_op jit(solution)/shard_map/all_gather | solution.py:96
  239.0 4.1 %fusion.4 = f32[2,256,1024]{2,1,0:T(8,128)S(1)} fusion(bf16[2,1024,256]{2,1,0:T(8,128)(2,1)} %all-gather.11.cloned.1.call-done, bf16[2,2,1024,1024]{3,2,0,1:T(8,128)(2,1)} %get-tuple-element.27), kind=kOutput, calls=%fused_computation.12 | convolution fusion | flops 1073741824 | bytes 7340032 | tf_op jit(solution)/shard_map/srn,sna->sra/dot_general | solution.py:11
  243.2 5.5 %fusion.12 = bf16[2,1,1024,256]{2,3,0,1:T(8,128)(2,1)S(1)} fusion(f32[2,256,1024]{2,1,0:T(8,128)} %fusion.5, bf16[2,1024,256]{2,1,0:T(8,128)(2,1)S(1)} %copy-done.10, bf16[2,2,1024,1024]{3,2,0,1:T(8,128)(2,1)} %get-tuple-element.27, f32[2,256,1024]{2,1,0:T(8,128)} %fusion.1, f32[2,256,1024]{2,1,0:T(8,128)S(1)} %copy-done.6, ...), kind=kOutput, calls=%fused_computation.25 | convolution fusion | flops 1076887552 | bytes 13631488 | tf_op jit(solution)/shard_map/srn,sna->sra/dot_general | solution.py:10
  249.3 2.2 fusion.13
  251.7 2.6 copy.106
  (84 shorter events, 4.7 us)
Async XLA Ops:
  7.2 120.3 %copy-start = (s32[256]{0:T(256)S(1)}, s32[256]{0:T(256)}, u32[]{:S(2)}) copy-start(s32[256]{0:T(256)} %param.17) | copy-start | bytes 3076
  7.2 4.1 %copy-start.19 = (bf16[2,2,1024,256]{3,2,1,0:T(8,128)(2,1)S(1)}, bf16[2,2,1024,256]{3,2,1,0:T(8,128)(2,1)}, u32[]{:S(2)}) copy-start(bf16[2,2,1024,256]{3,2,1,0:T(8,128)(2,1)} %param.12) | copy-start | bytes 6291460
  7.2 4.1 %copy-start.13 = (bf16[2,2,2,32,1024]{4,3,2,1,0:T(8,128)(2,1)S(1)}, bf16[2,2,2,32,1024]{4,3,2,1,0:T(8,128)(2,1)}, u32[]{:S(2)}) copy-start(bf16[2,2,2,32,1024]{4,3,2,1,0:T(8,128)(2,1)} %param.9) | copy-start | bytes 1572868
  7.2 188.4 %all-gather.7.cloned.1.call-start = ((), (), s32[]{:S(2)}) async-start(), calls=%async_computation.1 | async-start | bytes 1081344 | tf_op jit(solution)/shard_map/all_gather | solution.py:88
  9.0 3.6 %copy-start.8 = (bf16[2,2,32,1024]{3,2,1,0:T(8,128)(2,1)S(1)}, bf16[2,2,32,1024]{3,2,1,0:T(8,128)(2,1)}, u32[]{:S(2)}) copy-start(bf16[2,2,32,1024]{3,2,1,0:T(8,128)(2,1)} %param.10) | copy-start | bytes 786436
  11.2 1.4 copy-start.11
  11.3 194.6 %all-gather.5.cloned.1.call-start = ((), (), s32[]{:S(2)}) async-start(), calls=%async_computation | async-start | bytes 1081344 | tf_op jit(solution)/shard_map/all_gather | solution.py:87
  12.5 0.8 copy-start.12
  12.6 203.6 %all-gather.9.cloned.1.call-start = ((), (), s32[]{:S(2)}) async-start(), calls=%async_computation.2 | async-start | bytes 1081344 | tf_op jit(solution)/shard_map/all_gather | solution.py:95
  13.3 0.8 copy-start.16
  15.3 1.3 copy-start.2
  120.5 3.8 %copy-start.3 = (bf16[2,1024,256]{1,2,0:T(8,128)(2,1)S(1)}, bf16[2,1024,256]{1,2,0:T(8,128)(2,1)}, u32[]{:S(2)}) copy-start(bf16[2,1024,256]{1,2,0:T(8,128)(2,1)} %get-tuple-element.17) | copy-start | bytes 3145732
  120.5 3.8 %copy-start.14 = (bf16[2,2,2,32,1024]{4,3,2,1,0:T(8,128)(2,1)S(1)}, bf16[2,2,2,32,1024]{4,3,2,1,0:T(8,128)(2,1)}, u32[]{:S(2)}) copy-start(bf16[2,2,2,32,1024]{4,3,2,1,0:T(8,128)(2,1)} %param.9) | copy-start | bytes 1572868
  124.2 1.6 copy-start.15
  124.2 2.5 copy-start.17
  124.2 3.0 %copy-start.18 = (s32[2,32,3]{1,0,2:T(2,128)S(1)}, s32[2,32,3]{1,0,2:T(2,128)}, u32[]{:S(2)}) copy-start(s32[2,32,3]{1,0,2:T(2,128)} %param.16) | copy-start | bytes 2308
  124.2 114.8 %all-gather.11.cloned.1.call-start = ((), (), s32[]{:S(2)}) async-start(), calls=%async_computation.3 | async-start | bytes 1081344 | tf_op jit(solution)/shard_map/all_gather | solution.py:96
  170.2 11.8 %copy-start.4 = (bf16[2,2,1024,256]{3,2,1,0:T(8,128)(2,1)S(1)}, bf16[2,2,1024,256]{3,2,1,0:T(8,128)(2,1)}, u32[]{:S(2)}) copy-start(bf16[2,2,1024,256]{3,2,1,0:T(8,128)(2,1)} %param.14) | copy-start | bytes 6291460
  195.6 5.3 %copy-start.20 = (bf16[2,1024,256]{2,1,0:T(8,128)(2,1)S(1)}, bf16[2,1024,256]{2,1,0:T(8,128)(2,1)}, u32[]{:S(2)}) copy-start(bf16[2,1024,256]{2,1,0:T(8,128)(2,1)} %all-gather.7.cloned.1.call-done) | copy-start | bytes 3145732
  205.8 5.4 %copy-start.21 = (bf16[2,1024,256]{2,1,0:T(8,128)(2,1)S(1)}, bf16[2,1024,256]{2,1,0:T(8,128)(2,1)}, u32[]{:S(2)}) copy-start(bf16[2,1024,256]{2,1,0:T(8,128)(2,1)} %all-gather.5.cloned.1.call-done) | copy-start | bytes 3145732
  239.0 4.1 %copy-start.6 = (f32[2,256,1024]{2,1,0:T(8,128)S(1)}, f32[2,256,1024]{2,1,0:T(8,128)}, u32[]{:S(2)}) copy-start(f32[2,256,1024]{2,1,0:T(8,128)} %fusion.3) | copy-start | bytes 6291460
  239.0 4.1 %copy-start.10 = (bf16[2,1024,256]{2,1,0:T(8,128)(2,1)S(1)}, bf16[2,1024,256]{2,1,0:T(8,128)(2,1)}, u32[]{:S(2)}) copy-start(bf16[2,1024,256]{2,1,0:T(8,128)(2,1)} %all-gather.11.cloned.1.call-done) | copy-start | bytes 3145732
  239.0 9.6 %slice-start = ((s8[8388608]{0:T(1024)(128)(4,1)}), s8[4194304]{0:T(1024)(128)(4,1)S(1)}, s32[]{:S(2)}) async-start(s8[8388608]{0:T(1024)(128)(4,1)} %bitcast.171), calls=%async_computation.4 | async-start | bytes 8388608
  243.1 5.6 %slice-start.1 = ((s8[8388608]{0:T(1024)(128)(4,1)}), s8[4194304]{0:T(1024)(128)(4,1)S(1)}, s32[]{:S(2)}) async-start(s8[8388608]{0:T(1024)(128)(4,1)} %bitcast.171), calls=%async_computation.5 | async-start | bytes 8388608
  243.1 5.6 %copy-start.5 = (f32[2,256,1024]{2,1,0:T(8,128)S(1)}, f32[2,256,1024]{2,1,0:T(8,128)}, u32[]{:S(2)}) copy-start(f32[2,256,1024]{2,1,0:T(8,128)} %fusion) | copy-start | bytes 6291460
  243.1 5.9 %copy-start.7 = (f32[2,256,1024]{2,1,0:T(8,128)S(1)}, f32[2,256,1024]{2,1,0:T(8,128)}, u32[]{:S(2)}) copy-start(f32[2,256,1024]{2,1,0:T(8,128)} %fusion.2) | copy-start | bytes 6291460
  243.2 6.2 %copy-start.9 = (bf16[2,1024,256]{2,1,0:T(8,128)(2,1)S(1)}, bf16[2,1024,256]{2,1,0:T(8,128)(2,1)}, u32[]{:S(2)}) copy-start(bf16[2,1024,256]{2,1,0:T(8,128)(2,1)} %all-gather.9.cloned.1.call-done) | copy-start | bytes 3145732
  251.5 2.8 %copy-start.1 = (s32[256]{0:T(256)S(1)}, s32[256]{0:T(256)}, u32[]{:S(2)}) copy-start(s32[256]{0:T(256)} %param.17) | copy-start | bytes 3076
Sparse Core Ops, SparseCore 0:
  11.4 57.5 all-gather.6
  72.0 55.2 all-gather.4
  130.4 53.0 all-gather.8
  186.3 52.6 all-gather.10
where the time goes:
time: 261 us
  blocking collectives  140 us (54%)
  matrix products  49.8 us (19%)
  local copies, waits for them, and re-layouts  36.4 us (14%)
  waiting for transfers between devices  17.6 us (7%)
  between operations  14.2 us (5%)
  other arithmetic  2.63 us (1%)
    psum x1, blocking collectives, body(): lax.psum((embed_rows(-below_real, own_right[:, 0]), embed_rows(-below_ima...  101 us
    unnamed x1, blocking collectives  39.2 us
    all_gather x1, waiting for transfers between devices, body(): lax.all_gather(second_imag, ('row', 'col'), axis=1, tiled=True)  17.5 us
    dot_general x5, matrix products, complex_rows(): jnp.einsum(form, left_pair[1], right_pair[1], preferred_element_type=jnp....  14.5 us
    dot_general x5, matrix products, complex_rows(): jnp.einsum(form, left_pair[0], right_pair[0], preferred_element_type=jnp....  12.9 us
    slice x1, local copies, waits for them, and re-layouts, body(): first_factor = trail_factor[:, 0]  11.8 us
    squeeze x1, local copies, waits for them, and re-layouts, body(): second_factor = trail_factor[:, 1]  11.7 us
    dot_general x5, matrix products, complex_rows(): jnp.einsum(form, left_pair[0], right_pair[1], preferred_element_type=jnp....  11.6 us
  transfers between devices with their start and end apart: 4, of which 1 were waited for; matrix products, arithmetic and copies ran while one was open for 26% of the time, Pallas kernels for 0%

commit v1 on v0

v1 whole, which is shorter than its diff:
```python
import functools

import jax
import jax.numpy as jnp
from jax import lax
from jax.experimental import pallas as pl
from jax.experimental.pallas import tpu as pltpu
from jax.sharding import PartitionSpec as P

MESH = pl.DeviceIdType.MESH
F32 = jnp.float32
BF16 = jnp.bfloat16


def couple_partials(panel_solution, shape_tiles):
    forward = panel_solution[0].astype(jnp.float32)
    adjoint = panel_solution[1].astype(jnp.float32)
    coupling_real = jnp.sum(forward[:, 0] * adjoint[:, 0] - forward[:, 1] * adjoint[:, 1], axis=-1)
    coupling_imag = jnp.sum(forward[:, 0] * adjoint[:, 1] + forward[:, 1] * adjoint[:, 0], axis=-1)
    return -(shape_tiles[0] * coupling_real - shape_tiles[1] * coupling_imag)


def spread_vertices(partials, element_vertices, vertex_slot, vertex_count):
    values = jnp.transpose(
        partials.reshape(3, 3, partials.shape[1], partials.shape[2]), (1, 2, 3, 0)
    )
    slots = vertex_slot[element_vertices]
    empty = jnp.zeros((3, vertex_count), jnp.float32)
    return empty.at[:, slots.reshape(-1)].add(values.reshape(3, -1))


def stack_rows(top, bottom):
    if top.shape[0] % 16:
        return jnp.concatenate([top.astype(F32), bottom.astype(F32)], axis=0).astype(BF16)
    return jnp.concatenate([top, bottom], axis=0)


def kernel(dims, inv, below, second, rhs_hbm, factor_hbm, trail_hbm, panel_out, update_hbm,
           rhs, factor, trail, update, held, columns,
           rhs_sem, factor_sem, trail_sem, update_sem,
           sems, column_send, column_recv):
    nx, ny, nz = dims
    rows, cols = nx * 2, ny * nz
    n = rows * cols
    h = inv.shape[3]
    nb = inv.shape[4]
    angles = second.shape[3]
    steps = factor.shape[3] // trail_tile(factor.shape[3])
    tile = trail_tile(factor.shape[3])
    row, col = lax.axis_index("row"), lax.axis_index("col")
    x, core = row // 2, row % 2
    z, y = col // ny, col % ny
    me = row * cols + col
    sent = []

    loads = {}
    for s in range(2):
        loads["rhs", s] = pltpu.make_async_copy(rhs_hbm.at[s], rhs.at[s], rhs_sem.at[s])
        loads["rhs", s].start()

    barrier = pltpu.get_barrier_semaphore()

    def greet(k, carry):
        other = lax.rem(me + k, n)
        pl.semaphore_signal(barrier, inc=1, device_id=(other // cols, other % cols),
                            device_id_type=MESH)
        return carry

    lax.fori_loop(1, n, greet, 0)
    for t in range(2):
        for s in range(2):
            loads["factor", s, t] = pltpu.make_async_copy(
                factor_hbm.at[s, t], factor.at[s, t], factor_sem.at[s, t])
            loads["factor", s, t].start()
            if t == 0:
                loads["trail", s] = pltpu.make_async_copy(
                    trail_hbm.at[s], trail.at[s], trail_sem.at[s])
                loads["trail", s].start()

    def column_copy(target, source):
        return pltpu.make_async_remote_copy(
            src_ref=below.at[target], dst_ref=columns.at[source],
            send_sem=column_send.at[target], recv_sem=column_recv.at[source],
            device_id=(target // cols, target % cols), device_id_type=MESH)

    def remote(index, stage, k, region, target):
        copy = pltpu.make_async_remote_copy(
            src_ref=held.at[(index,) + region], dst_ref=held.at[(index,) + region],
            send_sem=sems.at[0, stage, index, k], recv_sem=sems.at[1, stage, index, k],
            device_id=target, device_id_type=MESH)
        return copy

    def send(index, stage, k, region, target):
        copy = remote(index, stage, k, region, target)
        copy.start()
        sent.append(copy)

    def receive(index, stage, k, region):
        remote(index, stage, k, region, (row, col)).wait_recv()

    every = slice(None)

    def spread(round_, s, make_block):
        indices = [(round_ * 2 + s) * 2 + p for p in range(2)]
        mate = (x * 2 + 1 - core, col)
        real, imag = make_block()
        for i, part in zip(indices, (real, imag)):
            held[i, x, core, z, y] = part.astype(held.dtype)
            for k in range(1, nz):
                send(i, 0, k, (x, core, z, y), (row, lax.rem(z + k, nz) * ny + y))
        yield
        for p, i in enumerate(indices):
            for k in range(1, nz):
                receive(i, 0, k, (x, core, lax.rem(z + nz - k, nz), y))
            line = (x, core, every, y)
            if p == 0:
                for k in range(1, ny):
                    send(i, 1, k, line, (row, z * ny + lax.rem(y + k, ny)))
            else:
                for k in range(1, nx):
                    send(i, 1, k, line, (lax.rem(x + k, nx) * 2 + core, col))
            send(i, 3, 0, line, mate)
        yield
        for p, i in enumerate(indices):
            if p == 0:
                got = [(x, core, every, lax.rem(y + ny - k, ny)) for k in range(1, ny)]
            else:
                got = [(lax.rem(x + nx - k, nx), core, every, y) for k in range(1, nx)]
            for k, region in enumerate(got):
                receive(i, 1, k + 1, region)
            if p == 0:
                for k in range(1, nx):
                    send(i, 2, k, (x, core), (lax.rem(x + k, nx) * 2 + core, col))
            else:
                for k in range(1, ny):
                    send(i, 2, k, (every, core, every, y), (row, z * ny + lax.rem(y + k, ny)))
            for k, region in enumerate(got):
                send(i, 3, 1 + k, region, mate)
        yield
        for p, i in enumerate(indices):
            if p == 0:
                got = [(lax.rem(x + nx - k, nx), core) for k in range(1, nx)]
            else:
                got = [(every, core, every, lax.rem(y + ny - k, ny)) for k in range(1, ny)]
            for k, region in enumerate(got):
                receive(i, 2, k + 1, region)
                base = ny if p == 0 else nx
                send(i, 3, base + k, region, mate)
        yield
        far = 1 - core
        for p, i in enumerate(indices):
            receive(i, 3, 0, (x, far, every, y))
            if p == 0:
                got = [(x, far, every, lax.rem(y + ny - k, ny)) for k in range(1, ny)]
                got += [(lax.rem(x + nx - k, nx), far) for k in range(1, nx)]
            else:
                got = [(lax.rem(x + nx - k, nx), far, every, y) for k in range(1, nx)]
                got += [(every, far, every, lax.rem(y + ny - k, ny)) for k in range(1, ny)]
            for k, region in enumerate(got):
                receive(i, 3, 1 + k, region)

    def gathered(round_, s, p):
        block = held[(round_ * 2 + s) * 2 + p]
        return block.reshape(nb, angles).astype(BF16)

    def dot(a, b):
        return jnp.dot(a, b, preferred_element_type=F32)

    def solve(s, panel, right):
        left = stack_rows(inv[s, panel, 0], inv[s, panel, 1])
        by_real, by_imag = dot(left, right[0]), dot(left, right[1])
        real = (by_real[:h] - by_imag[h:]).astype(BF16)
        imag = (by_imag[:h] + by_real[h:]).astype(BF16)
        panel_out[s, panel, 0] = real
        panel_out[s, panel, 1] = imag
        return real, imag

    def first_block(s):
        loads["rhs", s].wait()
        return solve(s, 0, (rhs[s, 0], rhs[s, 1]))

    def right_block(s):
        left = columns[...].astype(BF16).reshape(nb, columns.shape[2])
        products = [lax.dot_general(left, gathered(0, s, p), (((0,), (0,)), ((), ())),
                                    preferred_element_type=F32) for p in range(2)]
        a, b = 2 * s * h, (2 * s + 1) * h
        real = products[0][a:a + h] - products[1][b:b + h]
        imag = products[1][a:a + h] + products[0][b:b + h]
        return (second[s, 0].astype(F32) - real).astype(BF16), (
            second[s, 1].astype(F32) - imag).astype(BF16)

    def second_block(s):
        return solve(s, 1, (gathered(1, s, 0), gathered(1, s, 1)))

    def trail_part(s, t, part):
        at = pl.ds(part * tile, tile)
        solved = [gathered(2 * t, s, p) for p in range(2)]
        fr, fi = factor[s, t, 0, at, :], factor[s, t, 1, at, :]
        real = dot(fr, solved[0]) - dot(fi, solved[1])
        imag = dot(fr, solved[1]) + dot(fi, solved[0])
        if t == 0:
            update[s, 0, at, :] = trail[s, 0, at, :].astype(F32) - real
            update[s, 1, at, :] = trail[s, 1, at, :].astype(F32) - imag
        else:
            trail[s, 0, at, :] = (update[s, 0, at, :] - real).astype(BF16)
            trail[s, 1, at, :] = (update[s, 1, at, :] - imag).astype(BF16)

    def trail_run(s, t, first, last):
        if first == 0:
            loads["factor", s, t].wait()
            if t == 0:
                loads["trail", s].wait()
        for part in range(first, last):
            trail_part(s, t, part)

    def chain(s):
        yield from spread(0, s, lambda: first_block(s))
        yield from spread(1, s, lambda: right_block(s))
        yield from spread(2, s, lambda: second_block(s))

    columns[me] = below[me]
    pl.semaphore_wait(barrier, n - 1)

    chains = [chain(0), chain(1)]
    next(chains[0])
    next(chains[1])

    def scatter(k, carry):
        column_copy(lax.rem(me + k, n), me).start()
        return carry

    lax.fori_loop(1, n, scatter, 0)
    next(chains[0])
    next(chains[1])
    next(chains[0])
    next(chains[1])
    next(chains[0])

    def collect(k, carry):
        column_copy(lax.rem(me + k, n), lax.rem(me + n - k, n)).wait()
        return carry

    lax.fori_loop(1, n, collect, 0)
    half = steps // 2
    next(chains[0])
    next(chains[1])
    next(chains[0])
    next(chains[1])
    trail_run(0, 0, 0, half)
    next(chains[0])
    next(chains[1])
    trail_run(0, 0, half, steps)
    next(chains[0])
    next(chains[1])
    next(chains[0])
    next(chains[1])
    next(chains[0])
    next(chains[1])
    trail_run(1, 0, 0, half)
    next(chains[0])
    next(chains[1])
    trail_run(1, 0, half, steps)
    next(chains[0])
    next(chains[1])
    next(chains[0], None)
    next(chains[1])
    stores = []
    trail_run(0, 1, 0, steps)
    stores.append(pltpu.make_async_copy(trail.at[0], update_hbm.at[0], update_sem.at[0]))
    stores[0].start()
    next(chains[1], None)
    trail_run(1, 1, 0, steps)
    stores.append(pltpu.make_async_copy(trail.at[1], update_hbm.at[1], update_sem.at[1]))
    stores[1].start()
    for copy in sent:
        copy.wait_send()
    for copy in stores:
        copy.wait()


def trail_tile(count):
    return min(count, 256)


def body(dims, panel_inverse, panel_below, trail_factor, first_rhs, second_rhs, trail_rhs,
         shape_tiles, element_vertices, vertex_slot):
    nx, ny, nz = dims
    n = nx * 2 * ny * nz
    h, nb = panel_inverse.shape[3], panel_inverse.shape[4]
    angles = first_rhs.shape[3]
    count = trail_factor.shape[3]
    kind = BF16 if h % 16 == 0 else F32
    lanes = -(-4 * h // 128) * 128
    below = panel_below.reshape(2, 2, h, n, h).transpose(3, 2, 0, 1, 4).reshape(n, h, 4 * h)
    below = jnp.pad(below.astype(kind), ((0, 0), (0, 0), (0, lanes - 4 * h)))
    widest = max(nx, ny, nz, nx + ny)
    vmem = pl.BlockSpec(memory_space=pltpu.VMEM)
    hbm = pl.BlockSpec(memory_space=pl.ANY)
    panel_solution, trail_update = pl.pallas_call(
        functools.partial(kernel, dims),
        out_shape=(
            jax.ShapeDtypeStruct((2, 2, 2, h, angles), BF16),
            jax.ShapeDtypeStruct(trail_rhs.shape, BF16),
        ),
        in_specs=[vmem, vmem, vmem, hbm, hbm, hbm],
        out_specs=(vmem, hbm),
        scratch_shapes=[
            pltpu.VMEM(first_rhs.shape, BF16),
            pltpu.VMEM(trail_factor.shape, BF16),
            pltpu.VMEM(trail_rhs.shape, BF16),
            pltpu.VMEM(trail_rhs.shape, F32),
            pltpu.VMEM((12, nx, 2, nz, ny, h, angles), kind),
            pltpu.VMEM((n, h, lanes), kind),
            pltpu.SemaphoreType.DMA((2,)),
            pltpu.SemaphoreType.DMA((2, 2)),
            pltpu.SemaphoreType.DMA((2,)),
            pltpu.SemaphoreType.DMA((2,)),
            pltpu.SemaphoreType.DMA((2, 4, 12, widest)),
            pltpu.SemaphoreType.DMA((n,)),
            pltpu.SemaphoreType.DMA((n,)),
        ],
        compiler_params=pltpu.CompilerParams(
            collective_id=0, has_side_effects=True, vmem_limit_bytes=56 * 1024 * 1024
        ),
        cost_estimate=pl.CostEstimate(
            flops=32 * count * nb * angles, bytes_accessed=24 * 1024 * 1024, transcendentals=0
        ),
    )(panel_inverse, below, second_rhs, first_rhs, trail_factor, trail_rhs)
    partials = couple_partials(panel_solution, shape_tiles)
    dense_local = spread_vertices(partials, element_vertices, vertex_slot, vertex_slot.shape[0])
    vertex_gradient = lax.psum_scatter(dense_local, ("row", "col"), scatter_dimension=1, tiled=True)
    return (panel_solution, trail_update, vertex_gradient)


def solution(mesh):
    rows, cols = mesh.shape["row"], mesh.shape["col"]
    nx = max(rows // 2, 1)
    ny = nx if cols % nx == 0 else 1
    return jax.shard_map(
        functools.partial(body, (nx, ny, cols // ny)),
        mesh=mesh,
        in_specs=(
            P(None, None, None, ("row", "col"), None),
            P(None, None, ("row", "col"), None),
            P(None, None, None, ("row", "col"), None),
            P(),
            P(None, None, ("row", "col"), None),
            P(None, None, ("row", "col"), None),
            P(None, None, None, ("row", "col")),
            P(None, ("row", "col"), None),
            P(),
        ),
        out_specs=(
            P(None, None, None, ("row", "col"), None),
            P(None, None, ("row", "col"), None),
            P(None, ("row", "col")),
        ),
        check_vma=False,
    )
```

time: 261 us -> 121 us (0.46)
  blocking collectives: 140 us -> 39.7 us
  Pallas kernels: 0 us -> 69.4 us
  matrix products: 49.8 us -> 0 us
  local copies, waits for them, and re-layouts: 36.4 us -> 9.03 us
  waiting for transfers between devices: 17.6 us -> 0 us
  between operations: 14.2 us -> 0.8 us
    psum x1 -> x0, blocking collectives: 101 us -> none  [body(): lax.psum((embed_rows(-below_real, own_right[:, 0]), embed_rows(-below_ima...]
    pallas_call x0 -> x1, Pallas kernels: none -> 69.4 us  [body(): pl.pallas_call(functools.partial(kernel, dims), out_shape=(jax.ShapeDtype...]
    dot_general x20 -> x0, matrix products: 49.8 us -> none  [the longest x5 14.5 us: complex_rows(): jnp.einsum(form, left_pair[1], right_pair[1], preferred_element_type=jnp....]
    all_gather x4 -> x0, waiting for transfers between devices: 17.5 us -> none  [the longest x1 17.5 us: body(): lax.all_gather(second_imag, ('row', 'col'), axis=1, tiled=True)]
    slice x2 -> x0, local copies, waits for them, and re-layouts: 11.9 us -> none  [the longest x1 11.8 us: body(): first_factor = trail_factor[:, 0]]
    squeeze x1 -> x0, local copies, waits for them, and re-layouts: 11.7 us -> none  [body(): second_factor = trail_factor[:, 1]]
    unnamed x55 -> x14, local copies, waits for them, and re-layouts: 7.7 us -> 2.66 us
    reshape x0 -> x3, local copies, waits for them, and re-layouts: none -> 4.15 us  [body(): panel_below.reshape(2, 2, h, n, h).transpose(3, 2, 0, 1, 4)]
  transfers between devices with their start and end apart: 4 -> 0, of which waited for: 1 -> 0; matrix products, arithmetic and copies ran while one was open for 26% -> 0% of each run, Pallas kernels for 0% -> 0%
where the time goes in v1:
time: 121 us
  Pallas kernels  69.4 us (57%)
  blocking collectives  39.7 us (33%)
  local copies, waits for them, and re-layouts  9.03 us (7%)
  other arithmetic  2.27 us (2%)
    pallas_call x1, Pallas kernels, body(): pl.pallas_call(functools.partial(kernel, dims), out_shape=(jax.ShapeDtype...  69.4 us
    unnamed x1, blocking collectives  39.7 us
    reshape x3, local copies, waits for them, and re-layouts, body(): panel_below.reshape(2, 2, h, n, h).transpose(3, 2, 0, 1, 4)  4.15 us
    unnamed x14, local copies, waits for them, and re-layouts  2.66 us

profile of v1, /device:TPU:0, one launch (start us, length us, event | category | flops | bytes accessed | tf_op | source)
XLA Modules:
  0.0 121.2 jit_solution(5303518403951157094)
XLA Ops:
  0.6 0.0 copy-start
  0.6 1.8 %reshape.61 = bf16[2,2,32,32,32]{4,3,2,1,0:T(8,128)(2,1)S(1)} reshape(bf16[2,2,32,1024]{3,2,1,0:T(8,128)(2,1)} %param.10) | data formatting | bytes 524288 | tf_op jit(solution)/shard_map/reshape | solution.py:294
  2.5 1.1 copy.33
  3.6 1.2 %reshape.62.below = bf16[32,32,128]{2,1,0:T(8,128)(2,1)} reshape(bf16[32,32,2,2,32]{4,3,2,1,0:T(2,128)(2,1)S(1)} %bitcast.20) | data formatting | bytes 524288 | tf_op jit(solution)/shard_map/reshape | solution.py:294
  4.8 0.0 copy-start.3
  4.8 0.0 copy-start.4
  4.8 69.4 %shard_map.112 = (bf16[2,2,2,32,256]{4,3,2,1,0:T(8,128)(2,1)}, bf16[2,2,1024,256]{3,2,1,0:T(8,128)(2,1)}) custom-call(bf16[2,2,2,32,1024]{4,3,2,1,0:T(8,128)(2,1)} %inv.1, bf16[32,32,128]{2,1,0:T(8,128)(2,1)} %reshape.62.below, bf16[2,2,32,256]{3,2,1,0:T(8,128)(2,1)} %second.1, bf16[2,2,1024,256]{3,2,1,0:T(8,128)(2,1)} %rhs_hbm.1, ...), custom_call_target="tpu_custom_call" | custom-call | flops 8589934592 | bytes 25165824 | tf_op jit(solution)/shard_map/pallas_call | solution.py:299
  74.2 0.9 bitcast_convert_fusion.1
  75.1 0.1 subtract_reduce_fusion
  75.2 0.0 copy-done.3
  75.2 0.1 copy.29
  75.3 0.1 reshape.76
  75.5 0.1 copy.30
  75.6 0.0 copy-done.4
  75.6 0.1 copy.28
  75.7 0.1 reshape.69
  75.9 0.0 copy-done
  75.9 0.0 copy-start.2
  75.9 0.0 copy-start.1
  75.9 1.6 %gather_fusion = s32[192]{0:T(256)S(1)} fusion(s32[256]{0:T(256)S(1)} %copy-done, s32[1024]{0:T(1024)S(1)} %pad_clamp_fusion), kind=kCustom, calls=%fused_computation | custom fusion | bytes 2304 | tf_op jit(solution)/shard_map/gather | solution.py:27
  77.5 1.3 %scatter_custom_fusion = f32[3,256]{0,1:T(8,128)S(1)} fusion(s32[192]{0:T(256)S(1)} %bitcast.25, f32[192,3]{1,0:T(8,128)S(1)} %copy.30, f32[]{:T(128)} %constant.3.clone.1), kind=kCustom, calls=%fused_computation.7 | custom fusion | flops 576 | bytes 3076 | tf_op jit(solution)/shard_map/scatter-add | solution.py:29
  78.8 39.7 %all-reduce = f32[3,256]{0,1:T(8,128)S(1)} all-reduce(f32[3,256]{0,1:T(8,128)S(1)} %scatter_custom_fusion), channel_id=2, replica_groups=mesh['row'=4,'col'=8] {'row','col'}, use_global_device_ids=true, to_apply=%region_3.4.clone | all-reduce | flops 768 | bytes 6144
  118.6 0.7 copy.31
  119.2 0.0 copy-done.2
  119.2 0.7 copy.36
  119.9 0.0 copy-done.1
  119.9 1.3 %copy.37 = bf16[2,2,1024,256]{3,2,1,0:T(8,128)(2,1)} copy(bf16[2,2,1024,256]{3,2,1,0:T(8,128)(2,1)S(1)} %copy-done.1) | data formatting | bytes 4194304
  (6 shorter events, 0.0 us)
Async XLA Ops:
  0.6 75.3 %copy-start = (s32[256]{0:T(256)S(1)}, s32[256]{0:T(256)}, u32[]{:S(2)}) copy-start(s32[256]{0:T(256)} %param.17) | copy-start | bytes 3076
  4.8 70.4 %copy-start.3 = (f32[2,9,2,32]{3,2,1,0:T(2,128)S(1)}, f32[2,9,2,32]{3,2,1,0:T(2,128)}, u32[]{:S(2)}) copy-start(f32[2,9,2,32]{3,2,1,0:T(2,128)} %param.15) | copy-start | bytes 13828
  4.8 70.8 %copy-start.4 = (s32[2,32,3]{1,0,2:T(2,128)S(1)}, s32[2,32,3]{1,0,2:T(2,128)}, u32[]{:S(2)}) copy-start(s32[2,32,3]{1,0,2:T(2,128)} %param.16) | copy-start | bytes 2308
  75.9 43.3 %copy-start.2 = (bf16[2,2,2,32,256]{4,3,2,1,0:T(8,128)(2,1)S(1)}, bf16[2,2,2,32,256]{4,3,2,1,0:T(8,128)(2,1)}, u32[]{:S(2)}) copy-start(bf16[2,2,2,32,256]{4,3,2,1,0:T(8,128)(2,1)} %get-tuple-element.28) | copy-start | bytes 393220
  75.9 44.0 %copy-start.1 = (bf16[2,2,1024,256]{3,2,1,0:T(8,128)(2,1)S(1)}, bf16[2,2,1024,256]{3,2,1,0:T(8,128)(2,1)}, u32[]{:S(2)}) copy-start(bf16[2,2,1024,256]{3,2,1,0:T(8,128)(2,1)} %get-tuple-element.29) | copy-start | bytes 6291460

commit v2 on v1

--- a/solution.py
+++ b/solution.py
@@ -12,33 +12,33 @@
 BF16 = jnp.bfloat16
 
 
-def couple_partials(panel_solution, shape_tiles):
-    forward = panel_solution[0].astype(jnp.float32)
-    adjoint = panel_solution[1].astype(jnp.float32)
-    coupling_real = jnp.sum(forward[:, 0] * adjoint[:, 0] - forward[:, 1] * adjoint[:, 1], axis=-1)
-    coupling_imag = jnp.sum(forward[:, 0] * adjoint[:, 1] + forward[:, 1] * adjoint[:, 0], axis=-1)
-    return -(shape_tiles[0] * coupling_real - shape_tiles[1] * coupling_imag)
-
-
-def spread_vertices(partials, element_vertices, vertex_slot, vertex_count):
-    values = jnp.transpose(
-        partials.reshape(3, 3, partials.shape[1], partials.shape[2]), (1, 2, 3, 0)
-    )
-    slots = vertex_slot[element_vertices]
-    empty = jnp.zeros((3, vertex_count), jnp.float32)
-    return empty.at[:, slots.reshape(-1)].add(values.reshape(3, -1))
-
-
 def stack_rows(top, bottom):
     if top.shape[0] % 16:
         return jnp.concatenate([top.astype(F32), bottom.astype(F32)], axis=0).astype(BF16)
     return jnp.concatenate([top, bottom], axis=0)
 
 
-def kernel(dims, inv, below, second, rhs_hbm, factor_hbm, trail_hbm, panel_out, update_hbm,
-           rhs, factor, trail, update, held, columns,
+def split_columns(parts, kind):
+    h, width = parts[0].shape
+    per, groups = 128 // h, width // 128
+    wide = F32 if h % 16 else BF16
+    rows = [jnp.concatenate([part[:, 128 * g:128 * (g + 1)] for part in parts], axis=1)
+            for g in range(groups)]
+    left = jnp.concatenate([row.astype(wide) for row in rows], axis=0).astype(BF16)
+    source = lax.broadcasted_iota(jnp.int32, (512, per * 128), 0)
+    target = lax.broadcasted_iota(jnp.int32, (512, per * 128), 1)
+    lane = source % 128
+    match = (lane // h == target // 128) & (target % 128 == (source // 128) * h + lane % h)
+    moved = jnp.dot(left, jnp.where(match, 1.0, 0.0).astype(BF16), preferred_element_type=F32)
+    return [moved[g * h:(g + 1) * h, r * 128:(r + 1) * 128].astype(kind)
+            for g in range(groups) for r in range(per)]
+
+
+def kernel(dims, inv, below_in, second, shapes, corners, slots, rhs_hbm, factor_hbm, trail_hbm,
+           panel_out, update_hbm, vertex_out,
+           rhs, factor, trail, update, held, columns, below, dense, sums,
            rhs_sem, factor_sem, trail_sem, update_sem,
-           sems, column_send, column_recv):
+           sems, column_send, column_recv, dense_send, dense_recv):
     nx, ny, nz = dims
     rows, cols = nx * 2, ny * nz
     n = rows * cols
@@ -218,12 +218,67 @@
         yield from spread(1, s, lambda: right_block(s))
         yield from spread(2, s, lambda: second_block(s))
 
+    def vertex_copy(target, source):
+        return pltpu.make_async_remote_copy(
+            src_ref=dense.at[target], dst_ref=sums.at[source],
+            send_sem=dense_send.at[target], recv_sem=dense_recv.at[source],
+            device_id=(target // cols, target % cols), device_id_type=MESH)
+
+    def vertex_partials(t):
+        fr, fi = panel_out[0, t, 0].astype(F32), panel_out[0, t, 1].astype(F32)
+        ar, ai = panel_out[1, t, 0].astype(F32), panel_out[1, t, 1].astype(F32)
+        ones = jnp.ones((8, angles), F32)
+
+        def over_angles(values):
+            return lax.dot_general(ones, values, (((1,), (1,)), ((), ())),
+                                   precision=lax.Precision.HIGHEST,
+                                   preferred_element_type=F32)[:1]
+
+        real, imag = over_angles(fr * ar - fi * ai), over_angles(fr * ai + fi * ar)
+        place = lax.broadcasted_iota(jnp.int32, (h, slots.shape[1]), 1)
+        total = None
+        for c in range(3):
+            named = corners[t, :, c:c + 1] == place
+            slot = jnp.sum(jnp.where(named, slots[...], 0), axis=1, keepdims=True)
+            hot = jnp.where(slot == place, 1.0, 0.0).astype(F32)
+            at = pl.ds(3 * c, 3)
+            values = shapes[1, at, t, :] * imag - shapes[0, at, t, :] * real
+            term = jnp.dot(values, hot, precision=lax.Precision.HIGHEST,
+                           preferred_element_type=F32)
+            total = term if total is None else total + term
+        return total
+
+    def vertex_send():
+        total = vertex_partials(0) + vertex_partials(1)
+        count = total.shape[1]
+        flat = jnp.concatenate([total, jnp.zeros((125, count), F32)], axis=0)
+        dense[...] = flat.T.reshape(dense.shape)
+        sums[me] = dense[me]
+
+        def start(k, carry):
+            vertex_copy(lax.rem(me + k, n), me).start()
+            return carry
+
+        lax.fori_loop(1, n, start, 0)
+
+    def vertex_collect():
+        def wait(k, carry):
+            vertex_copy(lax.rem(me + k, n), lax.rem(me + n - k, n)).wait()
+            return carry
+
+        lax.fori_loop(1, n, wait, 0)
+        vertex_out[...] = jnp.sum(sums[...], axis=0).T[:3]
+
+    pl.semaphore_wait(barrier, n - 1)
+
+    chains = [chain(0), chain(1)]
+    next(chains[0])
+    next(chains[1])
+
+    parts = [below_in[i, p] for i in range(2) for p in range(2)]
+    for d, block in enumerate(split_columns(parts, below.dtype)):
+        below[d] = block
     columns[me] = below[me]
-    pl.semaphore_wait(barrier, n - 1)
-
-    chains = [chain(0), chain(1)]
-    next(chains[0])
-    next(chains[1])
 
     def scatter(k, carry):
         column_copy(lax.rem(me + k, n), me).start()
@@ -256,6 +311,7 @@
     next(chains[1])
     next(chains[0])
     next(chains[1])
+    vertex_send()
     trail_run(1, 0, 0, half)
     next(chains[0])
     next(chains[1])
@@ -272,6 +328,7 @@
     trail_run(1, 1, 0, steps)
     stores.append(pltpu.make_async_copy(trail.at[1], update_hbm.at[1], update_sem.at[1]))
     stores[1].start()
+    vertex_collect()
     for copy in sent:
         copy.wait_send()
     for copy in stores:
@@ -290,20 +347,20 @@
     angles = first_rhs.shape[3]
     count = trail_factor.shape[3]
     kind = BF16 if h % 16 == 0 else F32
-    lanes = -(-4 * h // 128) * 128
-    below = panel_below.reshape(2, 2, h, n, h).transpose(3, 2, 0, 1, 4).reshape(n, h, 4 * h)
-    below = jnp.pad(below.astype(kind), ((0, 0), (0, 0), (0, lanes - 4 * h)))
+    lanes = 128
+    slot_count = vertex_slot.shape[0]
     widest = max(nx, ny, nz, nx + ny)
     vmem = pl.BlockSpec(memory_space=pltpu.VMEM)
     hbm = pl.BlockSpec(memory_space=pl.ANY)
-    panel_solution, trail_update = pl.pallas_call(
+    return pl.pallas_call(
         functools.partial(kernel, dims),
         out_shape=(
             jax.ShapeDtypeStruct((2, 2, 2, h, angles), BF16),
             jax.ShapeDtypeStruct(trail_rhs.shape, BF16),
+            jax.ShapeDtypeStruct((3, slot_count // n), F32),
         ),
-        in_specs=[vmem, vmem, vmem, hbm, hbm, hbm],
-        out_specs=(vmem, hbm),
+        in_specs=[vmem] * 6 + [hbm] * 3,
+        out_specs=(vmem, hbm, vmem),
         scratch_shapes=[
             pltpu.VMEM(first_rhs.shape, BF16),
             pltpu.VMEM(trail_factor.shape, BF16),
@@ -311,11 +368,16 @@
             pltpu.VMEM(trail_rhs.shape, F32),
             pltpu.VMEM((12, nx, 2, nz, ny, h, angles), kind),
             pltpu.VMEM((n, h, lanes), kind),
+            pltpu.VMEM((n, h, lanes), kind),
+            pltpu.VMEM((n, slot_count // n, 128), F32),
+            pltpu.VMEM((n, slot_count // n, 128), F32),
             pltpu.SemaphoreType.DMA((2,)),
             pltpu.SemaphoreType.DMA((2, 2)),
             pltpu.SemaphoreType.DMA((2,)),
             pltpu.SemaphoreType.DMA((2,)),
             pltpu.SemaphoreType.DMA((2, 4, 12, widest)),
+            pltpu.SemaphoreType.DMA((n,)),
+            pltpu.SemaphoreType.DMA((n,)),
             pltpu.SemaphoreType.DMA((n,)),
             pltpu.SemaphoreType.DMA((n,)),
         ],
@@ -325,11 +387,8 @@
         cost_estimate=pl.CostEstimate(
             flops=32 * count * nb * angles, bytes_accessed=24 * 1024 * 1024, transcendentals=0
         ),
-    )(panel_inverse, below, second_rhs, first_rhs, trail_factor, trail_rhs)
-    partials = couple_partials(panel_solution, shape_tiles)
-    dense_local = spread_vertices(partials, element_vertices, vertex_slot, vertex_slot.shape[0])
-    vertex_gradient = lax.psum_scatter(dense_local, ("row", "col"), scatter_dimension=1, tiled=True)
-    return (panel_solution, trail_update, vertex_gradient)
+    )(panel_inverse, panel_below, second_rhs, shape_tiles, element_vertices,
+      vertex_slot.reshape(1, slot_count), first_rhs, trail_factor, trail_rhs)
 
 
 def solution(mesh):

time: 121 us -> 78.9 us (0.65)
  blocking collectives: 39.7 us -> 0 us
  local copies, waits for them, and re-layouts: 9.03 us -> 6.58 us
  other arithmetic: 2.27 us -> 0 us
  Pallas kernels: 69.4 us -> 71.5 us
    unnamed x1 -> x0, blocking collectives: 39.7 us -> none
    reshape x5 -> x0, local copies, waits for them, and re-layouts: 4.41 us -> none  [the longest x3 4.15 us: body(): panel_below.reshape(2, 2, h, n, h).transpose(3, 2, 0, 1, 4)]
    unnamed x14 -> x6, local copies, waits for them, and re-layouts: 2.66 us -> 6.58 us
    pallas_call x1, Pallas kernels: 69.4 us -> 71.5 us  [body(): pl.pallas_call(functools.partial(kernel, dims), out_shape=(jax.ShapeDtype...]
    gather x1 -> x0, local copies, waits for them, and re-layouts: 1.61 us -> none  [spread_vertices(): slots = vertex_slot[element_vertices]]
    scatter-add x1 -> x0, other arithmetic: 1.25 us -> none  [spread_vertices(): return empty.at[:, slots.reshape(-1)].add(values.reshape(3, -1))]
where the time goes in v2:
time: 78.9 us; the launch traced here: 78.7 us
  Pallas kernels  71.5 us (91%)
  local copies, waits for them, and re-layouts  6.58 us (8%)
    pallas_call x1, Pallas kernels, body(): pl.pallas_call(functools.partial(kernel, dims), out_shape=(jax.ShapeDtype...  71.5 us
    unnamed x6, local copies, waits for them, and re-layouts  6.58 us

profile of v2, /device:TPU:0, one launch (start us, length us, event | category | flops | bytes accessed | tf_op | source)
XLA Modules:
  0.0 78.7 jit_solution(5338863767666327402)
XLA Ops:
  0.6 1.4 %copy.12.corners = s32[2,32,3]{2,1,0:T(8,128)} copy(s32[2,32,3]{1,0,2:T(2,128)} %param.16) | data formatting | bytes 1536 | tf_op args[7]
  2.0 71.5 %shard_map.112 = (bf16[2,2,2,32,256]{4,3,2,1,0:T(8,128)(2,1)}, bf16[2,2,1024,256]{3,2,1,0:T(8,128)(2,1)}, f32[3,8]{1,0:T(4,128)}) custom-call(bf16[2,2,2,32,1024]{4,3,2,1,0:T(8,128)(2,1)} %inv.1, bf16[2,2,32,1024]{3,2,1,0:T(8,128)(2,1)} %below_in.1, bf16[2,2,32,256]{3,2,1,0:T(8,128)(2,1)} %second.1, f32[2,9,2,32]{3,2,1,0:T(2,128)} %shapes.1, ...), custom_call_target="tpu_custom_call" | custom-call | flops 8589934592 | bytes 25165824 | tf_op jit(solution)/shard_map/pallas_call | solution.py:355
  73.5 1.6 %copy.16 = bf16[2,2,2,32,256]{4,3,2,1,0:T(8,128)(2,1)} copy(bf16[2,2,2,32,256]{4,3,2,1,0:T(8,128)(2,1)} %get-tuple-element.6) | data formatting | bytes 262144
  75.1 0.0 copy-start
  75.1 3.0 %copy.17 = bf16[2,2,1024,256]{3,2,1,0:T(8,128)(2,1)} copy(bf16[2,2,1024,256]{3,2,1,0:T(8,128)(2,1)} %get-tuple-element.7) | data formatting | bytes 4194304
  78.1 0.0 copy-done
  78.1 0.6 copy.18
Async XLA Ops:
  75.1 3.0 %copy-start = (f32[3,8]{1,0:T(4,128)S(1)}, f32[3,8]{1,0:T(4,128)}, u32[]{:S(2)}) copy-start(f32[3,8]{1,0:T(4,128)} %get-tuple-element.8) | copy-start | bytes 292

commit v3 on v2

--- a/solution.py
+++ b/solution.py
@@ -36,7 +36,7 @@
 
 def kernel(dims, inv, below_in, second, shapes, corners, slots, rhs_hbm, factor_hbm, trail_hbm,
            panel_out, update_hbm, vertex_out,
-           rhs, factor, trail, update, held, columns, below, dense, sums,
+           rhs, factor, trail, update, held, columns, turned, below, dense, sums,
            rhs_sem, factor_sem, trail_sem, update_sem,
            sems, column_send, column_recv, dense_send, dense_recv):
     nx, ny, nz = dims
@@ -180,12 +180,10 @@
         return solve(s, 0, (rhs[s, 0], rhs[s, 1]))
 
     def right_block(s):
-        left = columns[...].astype(BF16).reshape(nb, columns.shape[2])
-        products = [lax.dot_general(left, gathered(0, s, p), (((0,), (0,)), ((), ())),
-                                    preferred_element_type=F32) for p in range(2)]
-        a, b = 2 * s * h, (2 * s + 1) * h
-        real = products[0][a:a + h] - products[1][b:b + h]
-        imag = products[1][a:a + h] + products[0][b:b + h]
+        left = turned[2 * s * h:2 * (s + 1) * h]
+        products = [dot(left, gathered(0, s, p)) for p in range(2)]
+        real = products[0][:h] - products[1][h:]
+        imag = products[1][:h] + products[0][h:]
         return (second[s, 0].astype(F32) - real).astype(BF16), (
             second[s, 1].astype(F32) - imag).astype(BF16)
 
@@ -214,7 +212,7 @@
             trail_part(s, t, part)
 
     def chain(s):
-        yield from spread(0, s, lambda: first_block(s))
+        yield from spread(0, s, lambda: firsts[s])
         yield from spread(1, s, lambda: right_block(s))
         yield from spread(2, s, lambda: second_block(s))
 
@@ -235,24 +233,26 @@
                                    preferred_element_type=F32)[:1]
 
         real, imag = over_angles(fr * ar - fi * ai), over_angles(fr * ai + fi * ar)
-        place = lax.broadcasted_iota(jnp.int32, (h, slots.shape[1]), 1)
+        count = slots.shape[1]
+        place = lax.broadcasted_iota(jnp.int32, (count, h), 0)
+        owner = jnp.broadcast_to(slots[...].astype(F32), (8, count)).T[:, :1]
         total = None
         for c in range(3):
-            named = corners[t, :, c:c + 1] == place
-            slot = jnp.sum(jnp.where(named, slots[...], 0), axis=1, keepdims=True)
-            hot = jnp.where(slot == place, 1.0, 0.0).astype(F32)
+            named = corners[c, t:t + 1, :] == place
+            slot = jnp.sum(jnp.where(named, owner, 0.0), axis=0, keepdims=True)
+            hot = jnp.where(slot == place.astype(F32), 1.0, 0.0)
             at = pl.ds(3 * c, 3)
             values = shapes[1, at, t, :] * imag - shapes[0, at, t, :] * real
-            term = jnp.dot(values, hot, precision=lax.Precision.HIGHEST,
-                           preferred_element_type=F32)
+            values = jnp.concatenate([values, jnp.zeros((125, h), F32)], axis=0)
+            term = lax.dot_general(hot, values, (((1,), (1,)), ((), ())),
+                                   precision=lax.Precision.HIGHEST,
+                                   preferred_element_type=F32)
             total = term if total is None else total + term
         return total
 
     def vertex_send():
         total = vertex_partials(0) + vertex_partials(1)
-        count = total.shape[1]
-        flat = jnp.concatenate([total, jnp.zeros((125, count), F32)], axis=0)
-        dense[...] = flat.T.reshape(dense.shape)
+        dense[...] = total.reshape(dense.shape)
         sums[me] = dense[me]
 
         def start(k, carry):
@@ -269,6 +269,7 @@
         lax.fori_loop(1, n, wait, 0)
         vertex_out[...] = jnp.sum(sums[...], axis=0).T[:3]
 
+    firsts = [first_block(s) for s in range(2)]
     pl.semaphore_wait(barrier, n - 1)
 
     chains = [chain(0), chain(1)]
@@ -296,6 +297,7 @@
         return carry
 
     lax.fori_loop(1, n, collect, 0)
+    turned[...] = columns[...].astype(F32).reshape(nb, columns.shape[2]).T.astype(BF16)
     half = steps // 2
     next(chains[0])
     next(chains[1])
@@ -311,16 +313,16 @@
     next(chains[1])
     next(chains[0])
     next(chains[1])
+    trail_run(1, 0, 0, half)
+    next(chains[0])
+    next(chains[1])
+    trail_run(1, 0, half, steps)
+    next(chains[0])
+    next(chains[1])
+    next(chains[0], None)
+    next(chains[1])
+    stores = []
     vertex_send()
-    trail_run(1, 0, 0, half)
-    next(chains[0])
-    next(chains[1])
-    trail_run(1, 0, half, steps)
-    next(chains[0])
-    next(chains[1])
-    next(chains[0], None)
-    next(chains[1])
-    stores = []
     trail_run(0, 1, 0, steps)
     stores.append(pltpu.make_async_copy(trail.at[0], update_hbm.at[0], update_sem.at[0]))
     stores[0].start()
@@ -359,7 +361,7 @@
             jax.ShapeDtypeStruct(trail_rhs.shape, BF16),
             jax.ShapeDtypeStruct((3, slot_count // n), F32),
         ),
-        in_specs=[vmem] * 6 + [hbm] * 3,
+        in_specs=[vmem] * 6 + [pl.BlockSpec(memory_space=pltpu.HBM)] * 3,
         out_specs=(vmem, hbm, vmem),
         scratch_shapes=[
             pltpu.VMEM(first_rhs.shape, BF16),
@@ -368,6 +370,7 @@
             pltpu.VMEM(trail_rhs.shape, F32),
             pltpu.VMEM((12, nx, 2, nz, ny, h, angles), kind),
             pltpu.VMEM((n, h, lanes), kind),
+            pltpu.VMEM((lanes, nb), BF16),
             pltpu.VMEM((n, h, lanes), kind),
             pltpu.VMEM((n, slot_count // n, 128), F32),
             pltpu.VMEM((n, slot_count // n, 128), F32),
@@ -382,12 +385,12 @@
             pltpu.SemaphoreType.DMA((n,)),
         ],
         compiler_params=pltpu.CompilerParams(
-            collective_id=0, has_side_effects=True, vmem_limit_bytes=56 * 1024 * 1024
+            collective_id=0, has_side_effects=True, vmem_limit_bytes=40 * 1024 * 1024
         ),
         cost_estimate=pl.CostEstimate(
             flops=32 * count * nb * angles, bytes_accessed=24 * 1024 * 1024, transcendentals=0
         ),
-    )(panel_inverse, panel_below, second_rhs, shape_tiles, element_vertices,
+    )(panel_inverse, panel_below, second_rhs, shape_tiles, element_vertices.transpose(2, 0, 1),
       vertex_slot.reshape(1, slot_count), first_rhs, trail_factor, trail_rhs)
 
 

time: 78.9 us -> 82.7 us (1.048)
  local copies, waits for them, and re-layouts: 6.58 us -> 10.6 us
    unnamed x6 -> x19, local copies, waits for them, and re-layouts: 6.58 us -> 10.6 us
where the time goes in v3:
time: 82.7 us; the launch traced here: 82.2 us
  Pallas kernels  70.9 us (86%)
  local copies, waits for them, and re-layouts  10.6 us (13%)
    pallas_call x1, Pallas kernels, body(): pl.pallas_call(functools.partial(kernel, dims), out_shape=(jax.ShapeDtype...  70.9 us
    unnamed x19, local copies, waits for them, and re-layouts  10.6 us

profile of v3, /device:TPU:0, one launch (start us, length us, event | category | flops | bytes accessed | tf_op | source)
XLA Modules:
  0.0 82.2 jit_solution(8065559082938751841)
XLA Ops:
  0.6 0.0 copy-start
  0.6 1.6 %copy-done = bf16[2,2,1024,256]{3,2,1,0:T(8,128)(2,1)S(1)} copy-done((bf16[2,2,1024,256]{3,2,1,0:T(8,128)(2,1)S(1)}, bf16[2,2,1024,256]{3,2,1,0:T(8,128)(2,1)}, u32[]{:S(2)}) %copy-start) | copy-done | bytes 2097176
  2.2 0.0 copy-start.1
  2.2 1.6 %copy-done.1 = bf16[2,2,1024,256]{3,2,1,0:T(8,128)(2,1)S(1)} copy-done((bf16[2,2,1024,256]{3,2,1,0:T(8,128)(2,1)S(1)}, bf16[2,2,1024,256]{3,2,1,0:T(8,128)(2,1)}, u32[]{:S(2)}) %copy-start.1) | copy-done | bytes 2097176
  3.8 0.0 copy-start.2
  3.8 1.0 %copy-done.2 = bf16[2,2,2,32,1024]{4,3,2,1,0:T(8,128)(2,1)S(1)} copy-done((bf16[2,2,2,32,1024]{4,3,2,1,0:T(8,128)(2,1)S(1)}, bf16[2,2,2,32,1024]{4,3,2,1,0:T(8,128)(2,1)}, u32[]{:S(2)}) %copy-start.2) | copy-done | bytes 524312
  4.9 0.0 copy-start.3
  4.9 0.9 %copy-done.3 = bf16[2,2,32,1024]{3,2,1,0:T(8,128)(2,1)S(1)} copy-done((bf16[2,2,32,1024]{3,2,1,0:T(8,128)(2,1)S(1)}, bf16[2,2,32,1024]{3,2,1,0:T(8,128)(2,1)}, u32[]{:S(2)}) %copy-start.3) | copy-done | bytes 262168
  5.8 0.0 copy-start.4
  5.8 0.8 %copy-done.4 = bf16[2,2,32,256]{3,2,1,0:T(8,128)(2,1)S(1)} copy-done((bf16[2,2,32,256]{3,2,1,0:T(8,128)(2,1)S(1)}, bf16[2,2,32,256]{3,2,1,0:T(8,128)(2,1)}, u32[]{:S(2)}) %copy-start.4) | copy-done | bytes 65560
  6.7 0.0 copy-start.5
  6.7 0.7 copy-done.5
  7.4 0.0 copy-start.6
  7.4 0.7 copy-done.6
  8.1 0.0 copy-start.7
  8.1 0.7 copy-done.7
  8.7 70.9 %shard_map.112 = (bf16[2,2,2,32,256]{4,3,2,1,0:T(8,128)(2,1)S(1)}, bf16[2,2,1024,256]{3,2,1,0:T(8,128)(2,1)S(1)}, f32[3,8]{1,0:T(4,128)S(1)}) custom-call(bf16[2,2,2,32,1024]{4,3,2,1,0:T(8,128)(2,1)S(1)} %copy-done.2, bf16[2,2,32,1024]{3,2,1,0:T(8,128)(2,1)S(1)} %copy-done.3, bf16[2,2,32,256]{3,2,1,0:T(8,128)(2,1)S(1)} %copy-done.4, ...), custom_call_target="tpu_custom_call" | custom-call | flops 8589934592 | bytes 25165824 | tf_op jit(solution)/shard_map/pallas_call | solution.py:357
  79.7 0.7 copy.15
  80.3 1.3 %copy.16 = bf16[2,2,1024,256]{3,2,1,0:T(8,128)(2,1)} copy(bf16[2,2,1024,256]{3,2,1,0:T(8,128)(2,1)S(1)} %get-tuple-element.7) | data formatting | bytes 4194304
  81.7 0.6 copy.17
Async XLA Ops:
  0.6 1.6 %copy-start = (bf16[2,2,1024,256]{3,2,1,0:T(8,128)(2,1)S(1)}, bf16[2,2,1024,256]{3,2,1,0:T(8,128)(2,1)}, u32[]{:S(2)}) copy-start(bf16[2,2,1024,256]{3,2,1,0:T(8,128)(2,1)} %rhs_hbm.1) | copy-start | bytes 6291460
  2.2 1.6 %copy-start.1 = (bf16[2,2,1024,256]{3,2,1,0:T(8,128)(2,1)S(1)}, bf16[2,2,1024,256]{3,2,1,0:T(8,128)(2,1)}, u32[]{:S(2)}) copy-start(bf16[2,2,1024,256]{3,2,1,0:T(8,128)(2,1)} %trail_hbm.1) | copy-start | bytes 6291460
  3.8 1.0 %copy-start.2 = (bf16[2,2,2,32,1024]{4,3,2,1,0:T(8,128)(2,1)S(1)}, bf16[2,2,2,32,1024]{4,3,2,1,0:T(8,128)(2,1)}, u32[]{:S(2)}) copy-start(bf16[2,2,2,32,1024]{4,3,2,1,0:T(8,128)(2,1)} %inv.1) | copy-start | bytes 1572868
  4.9 0.9 %copy-start.3 = (bf16[2,2,32,1024]{3,2,1,0:T(8,128)(2,1)S(1)}, bf16[2,2,32,1024]{3,2,1,0:T(8,128)(2,1)}, u32[]{:S(2)}) copy-start(bf16[2,2,32,1024]{3,2,1,0:T(8,128)(2,1)} %below_in.1) | copy-start | bytes 786436
  5.8 0.8 %copy-start.4 = (bf16[2,2,32,256]{3,2,1,0:T(8,128)(2,1)S(1)}, bf16[2,2,32,256]{3,2,1,0:T(8,128)(2,1)}, u32[]{:S(2)}) copy-start(bf16[2,2,32,256]{3,2,1,0:T(8,128)(2,1)} %second.1) | copy-start | bytes 196612
  6.7 0.7 copy-start.5
  7.4 0.7 copy-start.6
  8.1 0.7 copy-start.7

commit v4 on v3

--- a/solution.py
+++ b/solution.py
@@ -274,8 +274,6 @@
 
     chains = [chain(0), chain(1)]
     next(chains[0])
-    next(chains[1])
-
     parts = [below_in[i, p] for i in range(2) for p in range(2)]
     for d, block in enumerate(split_columns(parts, below.dtype)):
         below[d] = block
@@ -289,8 +287,8 @@
     next(chains[0])
     next(chains[1])
     next(chains[0])
+    next(chains[0])
     next(chains[1])
-    next(chains[0])
 
     def collect(k, carry):
         column_copy(lax.rem(me + k, n), lax.rem(me + n - k, n)).wait()
@@ -298,32 +296,28 @@
 
     lax.fori_loop(1, n, collect, 0)
     turned[...] = columns[...].astype(F32).reshape(nb, columns.shape[2]).T.astype(BF16)
-    half = steps // 2
-    next(chains[0])
-    next(chains[1])
-    next(chains[0])
-    next(chains[1])
-    trail_run(0, 0, 0, half)
-    next(chains[0])
-    next(chains[1])
-    trail_run(0, 0, half, steps)
-    next(chains[0])
-    next(chains[1])
-    next(chains[0])
-    next(chains[1])
-    next(chains[0])
-    next(chains[1])
-    trail_run(1, 0, 0, half)
-    next(chains[0])
-    next(chains[1])
-    trail_run(1, 0, half, steps)
-    next(chains[0])
-    next(chains[1])
+    cuts = [steps * k // 4 for k in range(5)]
+    for round_ in range(2):
+        next(chains[0])
+        next(chains[1])
+        trail_run(round_, 0, cuts[0], cuts[1])
+        next(chains[0])
+        next(chains[1])
+        trail_run(round_, 0, cuts[1], cuts[2])
+        next(chains[0])
+        next(chains[1])
+        trail_run(round_, 0, cuts[2], cuts[3])
+        next(chains[0])
+        next(chains[1])
+        if round_ == 1:
+            vertex_send()
+        trail_run(round_, 0, cuts[3], cuts[4])
+    stores = []
     next(chains[0], None)
     next(chains[1])
-    stores = []
-    vertex_send()
-    trail_run(0, 1, 0, steps)
+    trail_run(0, 1, cuts[0], cuts[2])
+    next(chains[1])
+    trail_run(0, 1, cuts[2], cuts[4])
     stores.append(pltpu.make_async_copy(trail.at[0], update_hbm.at[0], update_sem.at[0]))
     stores[0].start()
     next(chains[1], None)
@@ -361,7 +355,7 @@
             jax.ShapeDtypeStruct(trail_rhs.shape, BF16),
             jax.ShapeDtypeStruct((3, slot_count // n), F32),
         ),
-        in_specs=[vmem] * 6 + [pl.BlockSpec(memory_space=pltpu.HBM)] * 3,
+        in_specs=[vmem] * 6 + [hbm] * 3,
         out_specs=(vmem, hbm, vmem),
         scratch_shapes=[
             pltpu.VMEM(first_rhs.shape, BF16),
@@ -385,7 +379,7 @@
             pltpu.SemaphoreType.DMA((n,)),
         ],
         compiler_params=pltpu.CompilerParams(
-            collective_id=0, has_side_effects=True, vmem_limit_bytes=40 * 1024 * 1024
+            collective_id=0, has_side_effects=True, vmem_limit_bytes=56 * 1024 * 1024
         ),
         cost_estimate=pl.CostEstimate(
             flops=32 * count * nb * angles, bytes_accessed=24 * 1024 * 1024, transcendentals=0

time: 82.7 us -> 76.8 us (0.929)
  local copies, waits for them, and re-layouts: 10.6 us -> 5.19 us
    unnamed x19 -> x5, local copies, waits for them, and re-layouts: 10.6 us -> 5.19 us
where the time goes in v4:
time: 76.8 us; the launch traced here: 76.6 us
  Pallas kernels  70.8 us (92%)
  local copies, waits for them, and re-layouts  5.19 us (7%)
    pallas_call x1, Pallas kernels, body(): pl.pallas_call(functools.partial(kernel, dims), out_shape=(jax.ShapeDtype...  70.8 us
    unnamed x5, local copies, waits for them, and re-layouts  5.19 us

profile of v4, /device:TPU:0, one launch (start us, length us, event | category | flops | bytes accessed | tf_op | source)
XLA Modules:
  0.0 76.6 jit_solution(15916885094796869519)
XLA Ops:
  0.6 70.8 %shard_map.112 = (bf16[2,2,2,32,256]{4,3,2,1,0:T(8,128)(2,1)}, bf16[2,2,1024,256]{3,2,1,0:T(8,128)(2,1)}, f32[3,8]{1,0:T(4,128)}) custom-call(bf16[2,2,2,32,1024]{4,3,2,1,0:T(8,128)(2,1)} %inv.1, bf16[2,2,32,1024]{3,2,1,0:T(8,128)(2,1)} %below_in.1, bf16[2,2,32,256]{3,2,1,0:T(8,128)(2,1)} %second.1, f32[2,9,2,32]{3,2,1,0:T(2,128)} %shapes.1, ...), custom_call_target="tpu_custom_call" | custom-call | flops 8589934592 | bytes 25165824 | tf_op jit(solution)/shard_map/pallas_call | solution.py:351
  71.4 1.6 %copy.15 = bf16[2,2,2,32,256]{4,3,2,1,0:T(8,128)(2,1)} copy(bf16[2,2,2,32,256]{4,3,2,1,0:T(8,128)(2,1)} %get-tuple-element.6) | data formatting | bytes 262144
  73.0 0.0 copy-start
  73.0 3.0 %copy.16 = bf16[2,2,1024,256]{3,2,1,0:T(8,128)(2,1)} copy(bf16[2,2,1024,256]{3,2,1,0:T(8,128)(2,1)} %get-tuple-element.7) | data formatting | bytes 4194304
  76.0 0.0 copy-done
  76.0 0.6 copy.17
Async XLA Ops:
  73.0 3.0 %copy-start = (f32[3,8]{1,0:T(4,128)S(1)}, f32[3,8]{1,0:T(4,128)}, u32[]{:S(2)}) copy-start(f32[3,8]{1,0:T(4,128)} %get-tuple-element.8) | copy-start | bytes 292

commit v5 on v4

--- a/solution.py
+++ b/solution.py
@@ -27,8 +27,10 @@
     left = jnp.concatenate([row.astype(wide) for row in rows], axis=0).astype(BF16)
     source = lax.broadcasted_iota(jnp.int32, (512, per * 128), 0)
     target = lax.broadcasted_iota(jnp.int32, (512, per * 128), 1)
-    lane = source % 128
-    match = (lane // h == target // 128) & (target % 128 == (source // 128) * h + lane % h)
+    shift = h.bit_length() - 1
+    lane = source & 127
+    goal = (lane & (h - 1)) + ((source >> 7) << shift) + ((lane >> shift) << 7)
+    match = target == goal
     moved = jnp.dot(left, jnp.where(match, 1.0, 0.0).astype(BF16), preferred_element_type=F32)
     return [moved[g * h:(g + 1) * h, r * 128:(r + 1) * 128].astype(kind)
             for g in range(groups) for r in range(per)]
@@ -191,7 +193,7 @@
         return solve(s, 1, (gathered(1, s, 0), gathered(1, s, 1)))
 
     def trail_part(s, t, part):
-        at = pl.ds(part * tile, tile)
+        at = pl.ds(pl.multiple_of(part * tile, tile), tile)
         solved = [gathered(2 * t, s, p) for p in range(2)]
         fr, fi = factor[s, t, 0, at, :], factor[s, t, 1, at, :]
         real = dot(fr, solved[0]) - dot(fi, solved[1])
@@ -208,8 +210,12 @@
             loads["factor", s, t].wait()
             if t == 0:
                 loads["trail", s].wait()
-        for part in range(first, last):
+
+        def step(part, carry):
             trail_part(s, t, part)
+            return carry
+
+        lax.fori_loop(first, last, step, 0)
 
     def chain(s):
         yield from spread(0, s, lambda: firsts[s])
@@ -300,24 +306,21 @@
     for round_ in range(2):
         next(chains[0])
         next(chains[1])
-        trail_run(round_, 0, cuts[0], cuts[1])
+        trail_run(round_, 0, cuts[0], cuts[2])
         next(chains[0])
         next(chains[1])
-        trail_run(round_, 0, cuts[1], cuts[2])
         next(chains[0])
         next(chains[1])
-        trail_run(round_, 0, cuts[2], cuts[3])
+        trail_run(round_, 0, cuts[2], cuts[4])
         next(chains[0])
         next(chains[1])
         if round_ == 1:
             vertex_send()
-        trail_run(round_, 0, cuts[3], cuts[4])
     stores = []
     next(chains[0], None)
     next(chains[1])
-    trail_run(0, 1, cuts[0], cuts[2])
     next(chains[1])
-    trail_run(0, 1, cuts[2], cuts[4])
+    trail_run(0, 1, 0, steps)
     stores.append(pltpu.make_async_copy(trail.at[0], update_hbm.at[0], update_sem.at[0]))
     stores[0].start()
     next(chains[1], None)

time: 76.8 us -> 78.3 us (1.020)
  Pallas kernels: 70.8 us -> 72.2 us
    pallas_call x1, Pallas kernels: 70.8 us -> 72.2 us  [body(): pl.pallas_call(functools.partial(kernel, dims), out_shape=(jax.ShapeDtype...]
where the time goes in v5:
time: 78.3 us; the launch traced here: 78.1 us
  Pallas kernels  72.2 us (92%)
  local copies, waits for them, and re-layouts  5.19 us (7%)
    pallas_call x1, Pallas kernels, body(): pl.pallas_call(functools.partial(kernel, dims), out_shape=(jax.ShapeDtype...  72.2 us
    unnamed x5, local copies, waits for them, and re-layouts  5.19 us

profile of v5, /device:TPU:0, one launch (start us, length us, event | category | flops | bytes accessed | tf_op | source)
XLA Modules:
  0.0 78.1 jit_solution(16421191659276564897)
XLA Ops:
  0.6 72.2 %shard_map.112 = (bf16[2,2,2,32,256]{4,3,2,1,0:T(8,128)(2,1)}, bf16[2,2,1024,256]{3,2,1,0:T(8,128)(2,1)}, f32[3,8]{1,0:T(4,128)}) custom-call(bf16[2,2,2,32,1024]{4,3,2,1,0:T(8,128)(2,1)} %inv.1, bf16[2,2,32,1024]{3,2,1,0:T(8,128)(2,1)} %below_in.1, bf16[2,2,32,256]{3,2,1,0:T(8,128)(2,1)} %second.1, f32[2,9,2,32]{3,2,1,0:T(2,128)} %shapes.1, ...), custom_call_target="tpu_custom_call" | custom-call | flops 8589934592 | bytes 25165824 | tf_op jit(solution)/shard_map/pallas_call | solution.py:354
  72.9 1.6 %copy.15 = bf16[2,2,2,32,256]{4,3,2,1,0:T(8,128)(2,1)} copy(bf16[2,2,2,32,256]{4,3,2,1,0:T(8,128)(2,1)} %get-tuple-element.6) | data formatting | bytes 262144
  74.4 0.0 copy-start
  74.4 3.0 %copy.16 = bf16[2,2,1024,256]{3,2,1,0:T(8,128)(2,1)} copy(bf16[2,2,1024,256]{3,2,1,0:T(8,128)(2,1)} %get-tuple-element.7) | data formatting | bytes 4194304
  77.5 0.0 copy-done
  77.5 0.6 copy.17
Async XLA Ops:
  74.4 3.0 %copy-start = (f32[3,8]{1,0:T(4,128)S(1)}, f32[3,8]{1,0:T(4,128)}, u32[]{:S(2)}) copy-start(f32[3,8]{1,0:T(4,128)} %get-tuple-element.8) | copy-start | bytes 292

commit v6 on v4

--- a/solution.py
+++ b/solution.py
@@ -27,8 +27,10 @@
     left = jnp.concatenate([row.astype(wide) for row in rows], axis=0).astype(BF16)
     source = lax.broadcasted_iota(jnp.int32, (512, per * 128), 0)
     target = lax.broadcasted_iota(jnp.int32, (512, per * 128), 1)
-    lane = source % 128
-    match = (lane // h == target // 128) & (target % 128 == (source // 128) * h + lane % h)
+    shift = h.bit_length() - 1
+    lane = source & 127
+    goal = (lane & (h - 1)) + ((source >> 7) << shift) + ((lane >> shift) << 7)
+    match = target == goal
     moved = jnp.dot(left, jnp.where(match, 1.0, 0.0).astype(BF16), preferred_element_type=F32)
     return [moved[g * h:(g + 1) * h, r * 128:(r + 1) * 128].astype(kind)
             for g in range(groups) for r in range(per)]
@@ -109,55 +111,26 @@
             for k in range(1, nz):
                 send(i, 0, k, (x, core, z, y), (row, lax.rem(z + k, nz) * ny + y))
         yield
-        for p, i in enumerate(indices):
+        plane = [(a, b) for a in range(nx) for b in range(ny) if (a, b) != (0, 0)]
+        for i in indices:
             for k in range(1, nz):
                 receive(i, 0, k, (x, core, lax.rem(z + nz - k, nz), y))
             line = (x, core, every, y)
-            if p == 0:
-                for k in range(1, ny):
-                    send(i, 1, k, line, (row, z * ny + lax.rem(y + k, ny)))
-            else:
-                for k in range(1, nx):
-                    send(i, 1, k, line, (lax.rem(x + k, nx) * 2 + core, col))
-            send(i, 3, 0, line, mate)
+            for k, (a, b) in enumerate(plane):
+                send(i, 1, k, line, (lax.rem(x + a, nx) * 2 + core, z * ny + lax.rem(y + b, ny)))
+            send(i, 2, 0, line, mate)
         yield
-        for p, i in enumerate(indices):
-            if p == 0:
-                got = [(x, core, every, lax.rem(y + ny - k, ny)) for k in range(1, ny)]
-            else:
-                got = [(lax.rem(x + nx - k, nx), core, every, y) for k in range(1, nx)]
-            for k, region in enumerate(got):
-                receive(i, 1, k + 1, region)
-            if p == 0:
-                for k in range(1, nx):
-                    send(i, 2, k, (x, core), (lax.rem(x + k, nx) * 2 + core, col))
-            else:
-                for k in range(1, ny):
-                    send(i, 2, k, (every, core, every, y), (row, z * ny + lax.rem(y + k, ny)))
-            for k, region in enumerate(got):
-                send(i, 3, 1 + k, region, mate)
+        for i in indices:
+            for k, (a, b) in enumerate(plane):
+                line = (lax.rem(x + nx - a, nx), core, every, lax.rem(y + ny - b, ny))
+                receive(i, 1, k, line)
+                send(i, 2, 1 + k, line, mate)
         yield
-        for p, i in enumerate(indices):
-            if p == 0:
-                got = [(lax.rem(x + nx - k, nx), core) for k in range(1, nx)]
-            else:
-                got = [(every, core, every, lax.rem(y + ny - k, ny)) for k in range(1, ny)]
-            for k, region in enumerate(got):
-                receive(i, 2, k + 1, region)
-                base = ny if p == 0 else nx
-                send(i, 3, base + k, region, mate)
-        yield
-        far = 1 - core
-        for p, i in enumerate(indices):
-            receive(i, 3, 0, (x, far, every, y))
-            if p == 0:
-                got = [(x, far, every, lax.rem(y + ny - k, ny)) for k in range(1, ny)]
-                got += [(lax.rem(x + nx - k, nx), far) for k in range(1, nx)]
-            else:
-                got = [(lax.rem(x + nx - k, nx), far, every, y) for k in range(1, nx)]
-                got += [(every, far, every, lax.rem(y + ny - k, ny)) for k in range(1, ny)]
-            for k, region in enumerate(got):
-                receive(i, 3, 1 + k, region)
+        for i in indices:
+            receive(i, 2, 0, (x, 1 - core, every, y))
+            for k, (a, b) in enumerate(plane):
+                line = (lax.rem(x + nx - a, nx), 1 - core, every, lax.rem(y + ny - b, ny))
+                receive(i, 2, 1 + k, line)
 
     def gathered(round_, s, p):
         block = held[(round_ * 2 + s) * 2 + p]
@@ -287,7 +260,6 @@
     next(chains[0])
     next(chains[1])
     next(chains[0])
-    next(chains[0])
     next(chains[1])
 
     def collect(k, carry):
@@ -299,12 +271,10 @@
     cuts = [steps * k // 4 for k in range(5)]
     for round_ in range(2):
         next(chains[0])
+        trail_run(round_, 0, cuts[0], cuts[1])
         next(chains[1])
-        trail_run(round_, 0, cuts[0], cuts[1])
         next(chains[0])
-        next(chains[1])
         trail_run(round_, 0, cuts[1], cuts[2])
-        next(chains[0])
         next(chains[1])
         trail_run(round_, 0, cuts[2], cuts[3])
         next(chains[0])
@@ -314,7 +284,6 @@
         trail_run(round_, 0, cuts[3], cuts[4])
     stores = []
     next(chains[0], None)
-    next(chains[1])
     trail_run(0, 1, cuts[0], cuts[2])
     next(chains[1])
     trail_run(0, 1, cuts[2], cuts[4])
@@ -345,7 +314,7 @@
     kind = BF16 if h % 16 == 0 else F32
     lanes = 128
     slot_count = vertex_slot.shape[0]
-    widest = max(nx, ny, nz, nx + ny)
+    widest = max(nz, nx * ny)
     vmem = pl.BlockSpec(memory_space=pltpu.VMEM)
     hbm = pl.BlockSpec(memory_space=pl.ANY)
     return pl.pallas_call(
@@ -372,7 +341,7 @@
             pltpu.SemaphoreType.DMA((2, 2)),
             pltpu.SemaphoreType.DMA((2,)),
             pltpu.SemaphoreType.DMA((2,)),
-            pltpu.SemaphoreType.DMA((2, 4, 12, widest)),
+            pltpu.SemaphoreType.DMA((2, 3, 12, widest)),
             pltpu.SemaphoreType.DMA((n,)),
             pltpu.SemaphoreType.DMA((n,)),
             pltpu.SemaphoreType.DMA((n,)),

time: 76.8 us -> 70.5 us (0.918)
  Pallas kernels: 70.8 us -> 64.5 us
    pallas_call x1, Pallas kernels: 70.8 us -> 64.5 us  [body(): pl.pallas_call(functools.partial(kernel, dims), out_shape=(jax.ShapeDtype...]
where the time goes in v6:
time: 70.5 us; the launch traced here: 70.3 us
  Pallas kernels  64.5 us (91%)
  local copies, waits for them, and re-layouts  5.19 us (7%)
    pallas_call x1, Pallas kernels, body(): pl.pallas_call(functools.partial(kernel, dims), out_shape=(jax.ShapeDtype...  64.5 us
    unnamed x5, local copies, waits for them, and re-layouts  5.19 us

profile of v6, /device:TPU:0, one launch (start us, length us, event | category | flops | bytes accessed | tf_op | source)
XLA Modules:
  0.0 70.3 jit_solution(7610242377341862934)
XLA Ops:
  0.6 64.5 %shard_map.112 = (bf16[2,2,2,32,256]{4,3,2,1,0:T(8,128)(2,1)}, bf16[2,2,1024,256]{3,2,1,0:T(8,128)(2,1)}, f32[3,8]{1,0:T(4,128)}) custom-call(bf16[2,2,2,32,1024]{4,3,2,1,0:T(8,128)(2,1)} %inv.1, bf16[2,2,32,1024]{3,2,1,0:T(8,128)(2,1)} %below_in.1, bf16[2,2,32,256]{3,2,1,0:T(8,128)(2,1)} %second.1, f32[2,9,2,32]{3,2,1,0:T(2,128)} %shapes.1, ...), custom_call_target="tpu_custom_call" | custom-call | flops 8589934592 | bytes 25165824 | tf_op jit(solution)/shard_map/pallas_call | solution.py:320
  65.1 1.6 %copy.15 = bf16[2,2,2,32,256]{4,3,2,1,0:T(8,128)(2,1)} copy(bf16[2,2,2,32,256]{4,3,2,1,0:T(8,128)(2,1)} %get-tuple-element.6) | data formatting | bytes 262144
  66.7 0.0 copy-start
  66.7 3.0 %copy.16 = bf16[2,2,1024,256]{3,2,1,0:T(8,128)(2,1)} copy(bf16[2,2,1024,256]{3,2,1,0:T(8,128)(2,1)} %get-tuple-element.7) | data formatting | bytes 4194304
  69.7 0.0 copy-done
  69.7 0.6 copy.17
Async XLA Ops:
  66.7 3.0 %copy-start = (f32[3,8]{1,0:T(4,128)S(1)}, f32[3,8]{1,0:T(4,128)}, u32[]{:S(2)}) copy-start(f32[3,8]{1,0:T(4,128)} %get-tuple-element.8) | copy-start | bytes 292
